TPU v7x, 32 devices: a whole 2x2x4 slice. The times are simulated.
32 devices in a mesh: grid: 2 (over x), rank: 4 (over y, core), term: 4 (over z).
Axes of the slice: x: 2, y: 2, z: 4, core: 2. Of those that a mesh axis runs over, the one named last changes fastest.
Arguments:
- rhs: float32 [128, 4, 256], P('rank', 'grid')
- coef: float32 [12, 4, 256], P('term', 'grid'), may hold values from 0.03 to 0.3
- env: float32 [12, 128, 128], P('term', 'rank'), as said below
Outputs:
- solution: float32 [128, 4, 256], P('rank', 'grid')
- residual: float32 [128, 4, 256], P('rank', 'grid')
Inputs may be any that keep to these rules, and one draw needn't show every extreme that they name: env[k] is a symmetric matrix for every k.
All inputs are finite; a program needn't handle non-finite values.
Results may differ from a plain program's by a relative error of at most 0.0003.
Values sent between devices are 32-bit elements; how exact they have to be, the bound alone decides.
A program may use at most 64 MiB of HBM per device.

v0:
```python
import jax
import jax.numpy as jnp
from jax import lax
from jax.sharding import PartitionSpec as P

ITERS = 4


def padded_2(block, sides, width):
    for axis, dim in sides:
        count = lax.axis_size(axis)
        forward = [(i, i + 1) for i in range(count - 1)]
        backward = [(target, source) for source, target in forward]
        low = lax.ppermute(
            lax.slice_in_dim(block, block.shape[dim] - width, None, axis=dim), axis, forward
        )
        high = lax.ppermute(lax.slice_in_dim(block, 0, width, axis=dim), axis, backward)
        block = jnp.concatenate([low, block, high], axis=dim)
    return block


def face_weights(padded):
    wide = jnp.pad(padded, ((0, 0), (0, 0), (1, 1)))
    centre = wide[:, 1:-1, 1:-1]
    face_up = 0.5 * (centre + wide[:, 2:, 1:-1])
    face_down = 0.5 * (centre + wide[:, :-2, 1:-1])
    face_right = 0.5 * (centre + wide[:, 1:-1, 2:])
    face_left = 0.5 * (centre + wide[:, 1:-1, :-2])
    return (face_up + face_down + face_right + face_left, face_up, face_down, face_right, face_left)


def apply_faces(field, faces):
    middle = field[..., 1:-1, :]
    sideways = jnp.pad(middle, [(0, 0)] * (middle.ndim - 1) + [(1, 1)])
    total, face_up, face_down, face_right, face_left = faces
    return (
        total * middle
        - face_up * field[..., 2:, :]
        - face_down * field[..., :-2, :]
        - face_right * sideways[..., 2:]
        - face_left * sideways[..., :-2]
    )


def shards(rhs, coef, env):
    coef_padded = padded_2(coef, (("grid", 1),), 1)
    faces = tuple((weights[:, None] for weights in face_weights(coef_padded)))

    def square_sum(vector):
        return lax.psum(jnp.sum(vector * vector), ("grid", "rank"))

    solution = jnp.zeros(rhs.shape, jnp.float32)
    residual = rhs
    direction = rhs
    norm_now = square_sum(residual)
    for step in range(ITERS):
        padded = padded_2(direction, (("grid", 1),), 1)
        stenciled = apply_faces(padded[None], faces)
        image = lax.psum_scatter(
            jnp.einsum("krs,krxy->sxy", env, stenciled, precision=lax.Precision.HIGHEST),
            "rank",
            scatter_dimension=0,
            tiled=True,
        )
        image = lax.psum(image, "term")
        alpha = norm_now / lax.psum(jnp.sum(direction * image), ("grid", "rank"))
        solution = solution + alpha * direction
        residual = residual - alpha * image
        norm_next = square_sum(residual)
        direction = residual + norm_next / norm_now * direction
        norm_now = norm_next
    return (solution, residual)


def solution(mesh):
    placed = (P("rank", "grid", None), P("term", "grid", None), P("term", "rank", None))
    return jax.shard_map(
        shards,
        mesh=mesh,
        in_specs=placed,
        out_specs=(P("rank", "grid", None), P("rank", "grid", None)),
        check_vma=False,
    )
```

profile of v0, /device:TPU:0, one launch (start us, length us, event | category | flops | bytes accessed | tf_op | source)
XLA Modules:
  0.0 443.1 jit_solution(13769848011755938709)
XLA Ops:
  7.2 0.8 fusion.103
  8.0 4.8 %collective-permute-start.1 = (f32[3,1,256]{2,1,0:T(1,128)S(1)}, f32[3,1,256]{2,1,0:T(1,128)S(1)}, u32[]{:S(2)}, u32[]{:S(2)}) collective-permute-start(f32[3,1,256]{2,1,0:T(1,128)S(1)} %get-tuple-element.49), channel_id=1, source_target_pairs={{0,16},{1,17},{2,18},{3,19},{4,20},{5,21},{6,22},{7,23},{8,24},{9,... | collective-permute-start | bytes 9224 | tf_op jit(solution)/shard_map/ppermute | solution.py:14
  12.8 1.3 collective-permute-start
  14.2 1.0 fusion.102
  15.1 4.5 %collective-permute-start.2 = (f32[32,1,256]{2,1,0:T(1,128)S(1)}, f32[32,1,256]{2,1,0:T(1,128)S(1)}, u32[]{:S(2)}, u32[]{:S(2)}) collective-permute-start(f32[32,1,256]{2,1,0:T(1,128)S(1)} %get-tuple-element.47), channel_id=1, source_target_pairs={{0,16},{1,17},{2,18},{3,19},{4,20},{5,21},{6,22},{7,23},{8,24},{9,... | collective-permute-start | bytes 98312 | tf_op jit(solution)/shard_map/ppermute | solution.py:14
  19.7 1.3 collective-permute-start.3
  21.3 4.2 collective-permute-done.3
  26.6 0.8 copy.46
  27.5 0.6 copy-done.7
  29.4 30.5 %all-reduce.27.cloned.1.call-done = f32[128,2,256]{2,1,0:T(2,128)} async-done(((f32[128,2,256]{2,1,0:T(2,128)}), f32[128,2,256]{2,1,0:T(2,128)}) %all-reduce.27.cloned.1.call-update) | async-done | bytes 262160
  59.9 1.5 constant_dynamic-slice_fusion.3
  61.4 35.5 %all-reduce.19.cloned.1.call-done = f32[32,2,256]{2,1,0:T(2,128)} async-done(((f32[32,2,256]{2,1,0:T(2,128)}), f32[32,2,256]{2,1,0:T(2,128)}) %all-reduce.19.cloned.1.call-update) | async-done | bytes 65552 | tf_op jit(solution)/shard_map/psum | solution.py:65
  96.9 1.6 multiply_reduce_fusion.6
  98.5 12.5 %all-reduce.9 = (f32[]{:T(128)}, f32[]{:T(128)}) all-reduce(f32[]{:T(128)} %get-tuple-element.5, f32[]{:T(128)} %get-tuple-element.4), channel_id=1, replica_groups=mesh['grid'=2,'rank'=4,'term'=4] {'grid','rank'}, use_global_device_ids=true, to_apply=%region_1.2 | all-reduce | flops 2 | bytes 16 | tf_op jit(solution)/shard_map/psum | solution.py:50
  112.3 0.7 multiply_reduce_fusion.5
  113.0 12.5 %psum.87 = f32[]{:T(128)} all-reduce(f32[]{:T(128)} %multiply_reduce_fusion.5), channel_id=1, replica_groups=mesh['grid'=2,'rank'=4,'term'=4] {'grid','rank'}, use_global_device_ids=true, to_apply=%region_7.8 | all-reduce | flops 1 | bytes 8 | tf_op jit(solution)/shard_map/psum | solution.py:50
  126.9 3.4 collective-permute-start.4
  130.3 1.3 collective-permute-start.5
  131.9 4.2 collective-permute-done.5
  136.9 0.8 copy.50
  137.8 30.0 %all-reduce.29.cloned.1.call-done = f32[128,2,256]{2,1,0:T(2,128)} async-done(((f32[128,2,256]{2,1,0:T(2,128)}), f32[128,2,256]{2,1,0:T(2,128)}) %all-reduce.29.cloned.1.call-update) | async-done | bytes 262160
  167.8 1.5 constant_dynamic-slice_fusion.2
  169.3 35.3 %all-reduce.21.cloned.1.call-done = f32[32,2,256]{2,1,0:T(2,128)} async-done(((f32[32,2,256]{2,1,0:T(2,128)}), f32[32,2,256]{2,1,0:T(2,128)}) %all-reduce.21.cloned.1.call-update) | async-done | bytes 65552 | tf_op jit(solution)/shard_map/psum | solution.py:65
  204.6 1.6 multiply_reduce_fusion.4
  206.2 12.5 %psum.89 = f32[]{:T(128)} all-reduce(f32[]{:T(128)} %multiply_reduce_fusion.4), channel_id=1, replica_groups=mesh['grid'=2,'rank'=4,'term'=4] {'grid','rank'}, use_global_device_ids=true, to_apply=%region_11.12 | all-reduce | flops 1 | bytes 8 | tf_op jit(solution)/shard_map/psum | solution.py:66
  220.1 0.7 multiply_reduce_fusion.3
  220.7 12.4 %psum.90 = f32[]{:T(128)} all-reduce(f32[]{:T(128)} %get-tuple-element.10), channel_id=1, replica_groups=mesh['grid'=2,'rank'=4,'term'=4] {'grid','rank'}, use_global_device_ids=true, to_apply=%region_13.14 | all-reduce | flops 1 | bytes 8 | tf_op jit(solution)/shard_map/psum | solution.py:50
  234.6 3.4 collective-permute-start.6
  238.0 1.3 collective-permute-start.7
  239.6 4.2 collective-permute-done.7
  244.6 0.8 copy.54
  245.5 30.0 %all-reduce.31.cloned.1.call-done = f32[128,2,256]{2,1,0:T(2,128)} async-done(((f32[128,2,256]{2,1,0:T(2,128)}), f32[128,2,256]{2,1,0:T(2,128)}) %all-reduce.31.cloned.1.call-update) | async-done | bytes 262160
  275.4 1.5 constant_dynamic-slice_fusion.1
  277.0 35.3 %all-reduce.23.cloned.1.call-done = f32[32,2,256]{2,1,0:T(2,128)} async-done(((f32[32,2,256]{2,1,0:T(2,128)}), f32[32,2,256]{2,1,0:T(2,128)}) %all-reduce.23.cloned.1.call-update) | async-done | bytes 65552 | tf_op jit(solution)/shard_map/psum | solution.py:65
  312.3 1.6 multiply_reduce_fusion.2
  313.9 12.5 %psum.92 = f32[]{:T(128)} all-reduce(f32[]{:T(128)} %multiply_reduce_fusion.2), channel_id=1, replica_groups=mesh['grid'=2,'rank'=4,'term'=4] {'grid','rank'}, use_global_device_ids=true, to_apply=%region_17.18 | all-reduce | flops 1 | bytes 8 | tf_op jit(solution)/shard_map/psum | solution.py:66
  327.7 0.7 multiply_reduce_fusion.1
  328.4 12.5 %psum.93 = f32[]{:T(128)} all-reduce(f32[]{:T(128)} %get-tuple-element.8), channel_id=1, replica_groups=mesh['grid'=2,'rank'=4,'term'=4] {'grid','rank'}, use_global_device_ids=true, to_apply=%region_19.20 | all-reduce | flops 1 | bytes 8 | tf_op jit(solution)/shard_map/psum | solution.py:50
  342.3 3.4 collective-permute-start.8
  345.7 1.3 collective-permute-start.9
  347.3 4.2 collective-permute-done.9
  352.3 0.8 copy.58
  353.2 30.0 %all-reduce.33.cloned.1.call-done = f32[128,2,256]{2,1,0:T(2,128)} async-done(((f32[128,2,256]{2,1,0:T(2,128)}), f32[128,2,256]{2,1,0:T(2,128)}) %all-reduce.33.cloned.1.call-update) | async-done | bytes 262160
  383.1 1.5 constant_dynamic-slice_fusion
  384.6 35.5 %all-reduce.25.cloned.1.call-done = f32[32,2,256]{2,1,0:T(2,128)} async-done(((f32[32,2,256]{2,1,0:T(2,128)}), f32[32,2,256]{2,1,0:T(2,128)}) %all-reduce.25.cloned.1.call-update) | async-done | bytes 65552 | tf_op jit(solution)/shard_map/psum | solution.py:65
  420.1 1.6 multiply_reduce_fusion
  421.7 12.5 %psum.95 = f32[]{:T(128)} all-reduce(f32[]{:T(128)} %multiply_reduce_fusion), channel_id=1, replica_groups=mesh['grid'=2,'rank'=4,'term'=4] {'grid','rank'}, use_global_device_ids=true, to_apply=%region_23.24 | all-reduce | flops 1 | bytes 8 | tf_op jit(solution)/shard_map/psum | solution.py:66
  435.6 0.7 multiply_subtract_fusion
  (81 shorter events, 5.6 us)
Async XLA Ops:
  7.2 18.8 %copy-start = (f32[3,32,128]{2,1,0:T(8,128)S(1)}, f32[3,32,128]{2,1,0:T(8,128)}, u32[]{:S(2)}) copy-start(f32[3,32,128]{2,1,0:T(8,128)} %param.5) | copy-start | bytes 147460
  7.2 52.7 %all-reduce.27.cloned.1.call-start = ((), (), s32[]{:S(2)}) async-start(), calls=%async_computation.4 | async-start | bytes 524288
  8.0 13.0 %collective-permute-start.1 = (f32[3,1,256]{2,1,0:T(1,128)S(1)}, f32[3,1,256]{2,1,0:T(1,128)S(1)}, u32[]{:S(2)}, u32[]{:S(2)}) collective-permute-start(f32[3,1,256]{2,1,0:T(1,128)S(1)} %get-tuple-element.49), channel_id=1, source_target_pairs={{0,16},{1,17},{2,18},{3,19},{4,20},{5,21},{6,22},{7,23},{8,24},{9,... | collective-permute-start | bytes 9224 | tf_op jit(solution)/shard_map/ppermute | solution.py:14
  12.8 8.2 %collective-permute-start = (f32[3,1,256]{2,1,0:T(1,128)S(1)}, f32[3,1,256]{2,1,0:T(1,128)S(1)}, u32[]{:S(2)}, u32[]{:S(2)}) collective-permute-start(f32[3,1,256]{2,1,0:T(1,128)S(1)} %get-tuple-element.50), channel_id=1, source_target_pairs={{16,0},{17,1},{18,2},{19,3},{20,4},{21,5},{22,6},{23,7},{24,8},{25... | collective-permute-start | bytes 9224 | tf_op jit(solution)/shard_map/ppermute | solution.py:17
  14.1 6.9 %copy-start.6 = (f32[3,2,256]{2,1,0:T(2,128)S(1)}, f32[3,2,256]{2,1,0:T(2,128)}, u32[]{:S(2)}) copy-start(f32[3,2,256]{2,1,0:T(2,128)} %param.4) | copy-start | bytes 18436
  15.1 6.1 %collective-permute-start.2 = (f32[32,1,256]{2,1,0:T(1,128)S(1)}, f32[32,1,256]{2,1,0:T(1,128)S(1)}, u32[]{:S(2)}, u32[]{:S(2)}) collective-permute-start(f32[32,1,256]{2,1,0:T(1,128)S(1)} %get-tuple-element.47), channel_id=1, source_target_pairs={{0,16},{1,17},{2,18},{3,19},{4,20},{5,21},{6,22},{7,23},{8,24},{9,... | collective-permute-start | bytes 98312 | tf_op jit(solution)/shard_map/ppermute | solution.py:14
  19.7 5.8 %collective-permute-start.3 = (f32[32,1,256]{2,1,0:T(1,128)S(1)}, f32[32,1,256]{2,1,0:T(1,128)S(1)}, u32[]{:S(2)}, u32[]{:S(2)}) collective-permute-start(f32[32,1,256]{2,1,0:T(1,128)S(1)} %get-tuple-element.48), channel_id=1, source_target_pairs={{16,0},{17,1},{18,2},{19,3},{20,4},{21,5},{22,6},{23,7},{24,8},{25... | collective-permute-start | bytes 98312 | tf_op jit(solution)/shard_map/ppermute | solution.py:17
  21.1 4.4 copy-start.1
  27.4 69.5 %all-reduce.19.cloned.1.call-start = ((), (), s32[]{:S(2)}) async-start(), calls=%async_computation | async-start | bytes 131072 | tf_op jit(solution)/shard_map/psum | solution.py:65
  27.5 0.7 copy-start.7
  61.4 106.4 %all-reduce.29.cloned.1.call-start = ((), (), s32[]{:S(2)}) async-start(), calls=%async_computation.5 | async-start | bytes 524288
  96.9 15.4 %copy-start.2 = (f32[32,2,256]{2,1,0:T(2,128)S(1)}, f32[32,2,256]{2,1,0:T(2,128)}, u32[]{:S(2)}) copy-start(f32[32,2,256]{2,1,0:T(2,128)} %all-reduce.19.cloned.1.call-done) | copy-start | bytes 196612
  126.9 4.9 %collective-permute-start.4 = (f32[32,1,256]{2,1,0:T(1,128)S(1)}, f32[32,1,256]{2,1,0:T(1,128)S(1)}, u32[]{:S(2)}, u32[]{:S(2)}) collective-permute-start(f32[32,1,256]{2,1,0:T(1,128)S(1)} %get-tuple-element.43), channel_id=1, source_target_pairs={{0,16},{1,17},{2,18},{3,19},{4,20},{5,21},{6,22},{7,23},{8,24},{9,... | collective-permute-start | bytes 98312 | tf_op jit(solution)/shard_map/ppermute | solution.py:14
  130.3 5.8 %collective-permute-start.5 = (f32[32,1,256]{2,1,0:T(1,128)S(1)}, f32[32,1,256]{2,1,0:T(1,128)S(1)}, u32[]{:S(2)}, u32[]{:S(2)}) collective-permute-start(f32[32,1,256]{2,1,0:T(1,128)S(1)} %get-tuple-element.44), channel_id=1, source_target_pairs={{16,0},{17,1},{18,2},{19,3},{20,4},{21,5},{22,6},{23,7},{24,8},{25... | collective-permute-start | bytes 98312 | tf_op jit(solution)/shard_map/ppermute | solution.py:17
  137.7 66.9 %all-reduce.21.cloned.1.call-start = ((), (), s32[]{:S(2)}) async-start(), calls=%async_computation.1 | async-start | bytes 131072 | tf_op jit(solution)/shard_map/psum | solution.py:65
  169.2 106.2 %all-reduce.31.cloned.1.call-start = ((), (), s32[]{:S(2)}) async-start(), calls=%async_computation.6 | async-start | bytes 524288
  204.6 15.4 %copy-start.4 = (f32[32,2,256]{2,1,0:T(2,128)S(1)}, f32[32,2,256]{2,1,0:T(2,128)}, u32[]{:S(2)}) copy-start(f32[32,2,256]{2,1,0:T(2,128)} %all-reduce.21.cloned.1.call-done) | copy-start | bytes 196612
  234.6 4.9 %collective-permute-start.6 = (f32[32,1,256]{2,1,0:T(1,128)S(1)}, f32[32,1,256]{2,1,0:T(1,128)S(1)}, u32[]{:S(2)}, u32[]{:S(2)}) collective-permute-start(f32[32,1,256]{2,1,0:T(1,128)S(1)} %get-tuple-element.39), channel_id=1, source_target_pairs={{0,16},{1,17},{2,18},{3,19},{4,20},{5,21},{6,22},{7,23},{8,24},{9,... | collective-permute-start | bytes 98312 | tf_op jit(solution)/shard_map/ppermute | solution.py:14
  238.0 5.8 %collective-permute-start.7 = (f32[32,1,256]{2,1,0:T(1,128)S(1)}, f32[32,1,256]{2,1,0:T(1,128)S(1)}, u32[]{:S(2)}, u32[]{:S(2)}) collective-permute-start(f32[32,1,256]{2,1,0:T(1,128)S(1)} %get-tuple-element.40), channel_id=1, source_target_pairs={{16,0},{17,1},{18,2},{19,3},{20,4},{21,5},{22,6},{23,7},{24,8},{25... | collective-permute-start | bytes 98312 | tf_op jit(solution)/shard_map/ppermute | solution.py:17
  245.4 66.9 %all-reduce.23.cloned.1.call-start = ((), (), s32[]{:S(2)}) async-start(), calls=%async_computation.2 | async-start | bytes 131072 | tf_op jit(solution)/shard_map/psum | solution.py:65
  276.9 106.2 %all-reduce.33.cloned.1.call-start = ((), (), s32[]{:S(2)}) async-start(), calls=%async_computation.7 | async-start | bytes 524288
  312.3 15.4 %copy-start.3 = (f32[32,2,256]{2,1,0:T(2,128)S(1)}, f32[32,2,256]{2,1,0:T(2,128)}, u32[]{:S(2)}) copy-start(f32[32,2,256]{2,1,0:T(2,128)} %all-reduce.23.cloned.1.call-done) | copy-start | bytes 196612
  342.3 4.9 %collective-permute-start.8 = (f32[32,1,256]{2,1,0:T(1,128)S(1)}, f32[32,1,256]{2,1,0:T(1,128)S(1)}, u32[]{:S(2)}, u32[]{:S(2)}) collective-permute-start(f32[32,1,256]{2,1,0:T(1,128)S(1)} %get-tuple-element.35), channel_id=1, source_target_pairs={{0,16},{1,17},{2,18},{3,19},{4,20},{5,21},{6,22},{7,23},{8,24},{9,... | collective-permute-start | bytes 98312 | tf_op jit(solution)/shard_map/ppermute | solution.py:14
  345.7 5.8 %collective-permute-start.9 = (f32[32,1,256]{2,1,0:T(1,128)S(1)}, f32[32,1,256]{2,1,0:T(1,128)S(1)}, u32[]{:S(2)}, u32[]{:S(2)}) collective-permute-start(f32[32,1,256]{2,1,0:T(1,128)S(1)} %get-tuple-element.36), channel_id=1, source_target_pairs={{16,0},{17,1},{18,2},{19,3},{20,4},{21,5},{22,6},{23,7},{24,8},{25... | collective-permute-start | bytes 98312 | tf_op jit(solution)/shard_map/ppermute | solution.py:17
  353.1 67.0 %all-reduce.25.cloned.1.call-start = ((), (), s32[]{:S(2)}) async-start(), calls=%async_computation.3 | async-start | bytes 131072 | tf_op jit(solution)/shard_map/psum | solution.py:65
  420.1 15.4 %copy-start.5 = (f32[32,2,256]{2,1,0:T(2,128)S(1)}, f32[32,2,256]{2,1,0:T(2,128)}, u32[]{:S(2)}) copy-start(f32[32,2,256]{2,1,0:T(2,128)} %all-reduce.25.cloned.1.call-done) | copy-start | bytes 196612
Sparse Core Ops, SparseCore 0:
  27.6 32.2 all-reduce.26
  62.9 33.9 all-reduce.18
  137.9 29.8 all-reduce.28
  170.6 33.9 all-reduce.20
  245.5 29.8 all-reduce.30
  278.3 33.9 all-reduce.22
  353.2 29.8 all-reduce.32
  386.1 33.9 all-reduce.24
where the time goes:
time: 444 us; the launch traced here: 443 us
  waiting for transfers between devices  280 us (63%)
  blocking collectives  87.3 us (20%)
  starting transfers between devices  26.2 us (6%)
  between operations  24.8 us (6%)
  local copies, waits for them, and re-layouts  13.1 us (3%)
  other arithmetic  9.37 us (2%)
    psum x4, waiting for transfers between devices, shards(): image = lax.psum(image, 'term')  142 us
    unnamed x12, waiting for transfers between devices  121 us
    psum x4, blocking collectives, square_sum(): return lax.psum(jnp.sum(vector * vector), ('grid', 'rank'))  49.9 us
    psum x3, blocking collectives, shards(): alpha = norm_now / lax.psum(jnp.sum(direction * image), ('grid', 'rank'))  37.4 us
    ppermute x5, starting transfers between devices, padded_2(): lax.ppermute(lax.slice_in_dim(block, block.shape[dim] - width, None, axis...  19.4 us
    ppermute x5, waiting for transfers between devices, padded_2(): lax.ppermute(lax.slice_in_dim(block, 0, width, axis=dim), axis, backward)  16.9 us
  transfers between devices with their start and end apart: 18, of which 15 were waited for; matrix products, arithmetic and copies ran while one was open for 0% of the time, Pallas kernels for 0%

commit v1 on v0

--- a/solution.py
+++ b/solution.py
@@ -62,7 +62,8 @@
             scatter_dimension=0,
             tiled=True,
         )
-        image = lax.psum(image, "term")
+        parts = lax.all_gather(image, "term")
+        image = jnp.sum(parts, axis=0)
         alpha = norm_now / lax.psum(jnp.sum(direction * image), ("grid", "rank"))
         solution = solution + alpha * direction
         residual = residual - alpha * image

time: 444 us -> 355 us (0.80)
  waiting for transfers between devices: 280 us -> 141 us
  blocking collectives: 87.3 us -> 142 us
    psum x4 -> x0, waiting for transfers between devices: 142 us -> none  [shards(): image = lax.psum(image, 'term')]
    all_gather x0 -> x4, blocking collectives: none -> 55.5 us  [shards(): parts = lax.all_gather(image, 'term')]
    unnamed x12 -> x8, waiting for transfers between devices: 121 us -> 124 us
  transfers between devices with their start and end apart: 18 -> 14, of which waited for: 15 -> 11; matrix products, arithmetic and copies ran while one was open for 0% -> 1% of each run, Pallas kernels for 0% -> 0%
where the time goes in v1:
time: 355 us; the launch traced here: 354 us
  blocking collectives  142 us (40%)
  waiting for transfers between devices  141 us (40%)
  starting transfers between devices  26.2 us (7%)
  between operations  24.2 us (7%)
  local copies, waits for them, and re-layouts  11.8 us (3%)
  other arithmetic  5.81 us (2%)
    unnamed x8, waiting for transfers between devices  124 us
    all_gather x4, blocking collectives, shards(): parts = lax.all_gather(image, 'term')  55.5 us
    psum x4, blocking collectives, square_sum(): return lax.psum(jnp.sum(vector * vector), ('grid', 'rank'))  49.6 us
    psum x3, blocking collectives, shards(): alpha = norm_now / lax.psum(jnp.sum(direction * image), ('grid', 'rank'))  37.2 us
    ppermute x5, starting transfers between devices, padded_2(): lax.ppermute(lax.slice_in_dim(block, block.shape[dim] - width, None, axis...  19.5 us
    ppermute x5, waiting for transfers between devices, padded_2(): lax.ppermute(lax.slice_in_dim(block, 0, width, axis=dim), axis, backward)  16.9 us
  transfers between devices with their start and end apart: 14, of which 11 were waited for; matrix products, arithmetic and copies ran while one was open for 1% of the time, Pallas kernels for 0%

profile of v1, /device:TPU:0, one launch (start us, length us, event | category | flops | bytes accessed | tf_op | source)
XLA Modules:
  0.0 354.2 jit_solution(17296107138982622128)
XLA Ops:
  7.2 0.8 fusion.103
  8.0 4.8 %collective-permute-start.1 = (f32[3,1,256]{2,1,0:T(1,128)S(1)}, f32[3,1,256]{2,1,0:T(1,128)S(1)}, u32[]{:S(2)}, u32[]{:S(2)}) collective-permute-start(f32[3,1,256]{2,1,0:T(1,128)S(1)} %get-tuple-element.47), channel_id=1, source_target_pairs={{0,16},{1,17},{2,18},{3,19},{4,20},{5,21},{6,22},{7,23},{8,24},{9,... | collective-permute-start | bytes 9224 | tf_op jit(solution)/shard_map/ppermute | solution.py:14
  12.8 1.3 collective-permute-start
  14.2 1.0 fusion.102
  15.1 4.5 %collective-permute-start.2 = (f32[32,1,256]{2,1,0:T(1,128)S(1)}, f32[32,1,256]{2,1,0:T(1,128)S(1)}, u32[]{:S(2)}, u32[]{:S(2)}) collective-permute-start(f32[32,1,256]{2,1,0:T(1,128)S(1)} %get-tuple-element.45), channel_id=1, source_target_pairs={{0,16},{1,17},{2,18},{3,19},{4,20},{5,21},{6,22},{7,23},{8,24},{9,... | collective-permute-start | bytes 98312 | tf_op jit(solution)/shard_map/ppermute | solution.py:14
  19.7 1.3 collective-permute-start.3
  21.3 4.2 %collective-permute-done.3 = f32[32,1,256]{2,1,0:T(1,128)S(1)} collective-permute-done((f32[32,1,256]{2,1,0:T(1,128)S(1)}, f32[32,1,256]{2,1,0:T(1,128)S(1)}, u32[]{:S(2)}, u32[]{:S(2)}) %collective-permute-start.3) | collective-permute-done | bytes 32800 | tf_op jit(solution)/shard_map/ppermute | solution.py:17
  26.0 0.6 convolution_bitcast_fusion.3
  26.6 0.8 copy.69
  27.5 0.6 copy-done.3
  29.4 0.7 multiply_reduce_fusion.7
  30.1 29.8 %all-reduce.15.cloned.1.call-done = f32[128,2,256]{2,1,0:T(2,128)} async-done(((f32[128,2,256]{2,1,0:T(2,128)}), f32[128,2,256]{2,1,0:T(2,128)}) %all-reduce.15.cloned.1.call-update) | async-done | bytes 262160
  59.9 0.8 constant_dynamic-slice_fusion.3
  60.7 13.9 %all-gather = f32[128,2,256]{2,1,0:T(2,128)S(1)} all-gather(f32[32,2,256]{2,1,0:T(2,128)S(1)} %constant_dynamic-slice_fusion.3), channel_id=2, replica_groups=mesh['grid'=2,'rank'=4,'term'=4] {'term'}, dimensions={0}, use_global_device_ids=true | all-gather | bytes 327680 | tf_op jit(solution)/shard_map/all_gather | solution.py:65
  75.3 12.4 %all-reduce.9 = (f32[]{:T(128)}, f32[]{:T(128)}) all-reduce(f32[]{:T(128)} %multiply_reduce_fusion.7, f32[]{:T(128)} %multiply_reduce_fusion.6), channel_id=1, replica_groups=mesh['grid'=2,'rank'=4,'term'=4] {'grid','rank'}, use_global_device_ids=true, to_apply=%region_1.2 | all-reduce | flops 2 | bytes 16 | tf_op jit(solution)/shard_map/psum | solution.py:50
  89.7 12.4 %psum.58 = f32[]{:T(128)} all-reduce(f32[]{:T(128)} %multiply_reduce_fusion.5), channel_id=1, replica_groups=mesh['grid'=2,'rank'=4,'term'=4] {'grid','rank'}, use_global_device_ids=true, to_apply=%region_7.8 | all-reduce | flops 1 | bytes 8 | tf_op jit(solution)/shard_map/psum | solution.py:50
  103.5 3.4 collective-permute-start.4
  106.9 1.3 collective-permute-start.5
  108.5 4.2 %collective-permute-done.5 = f32[32,1,256]{2,0,1:T(8,128)S(1)} collective-permute-done((f32[32,1,256]{2,0,1:T(8,128)S(1)}, f32[32,1,256]{2,0,1:T(8,128)S(1)}, u32[]{:S(2)}, u32[]{:S(2)}) %collective-permute-start.5) | collective-permute-done | bytes 32800 | tf_op jit(solution)/shard_map/ppermute | solution.py:17
  112.9 0.6 convolution_bitcast_fusion.2
  113.5 0.8 copy.75
  114.4 31.2 %all-reduce.17.cloned.1.call-done = f32[128,2,256]{2,1,0:T(2,128)} async-done(((f32[128,2,256]{2,1,0:T(2,128)}), f32[128,2,256]{2,1,0:T(2,128)}) %all-reduce.17.cloned.1.call-update) | async-done | bytes 262160
  145.6 0.8 constant_dynamic-slice_fusion.2
  146.5 13.9 %all-gather.1 = f32[128,2,256]{2,1,0:T(2,128)S(1)} all-gather(f32[32,2,256]{2,1,0:T(2,128)S(1)} %constant_dynamic-slice_fusion.2), channel_id=3, replica_groups=mesh['grid'=2,'rank'=4,'term'=4] {'term'}, dimensions={0}, use_global_device_ids=true | all-gather | bytes 327680 | tf_op jit(solution)/shard_map/all_gather | solution.py:65
  161.1 12.4 %psum.59 = f32[]{:T(128)} all-reduce(f32[]{:T(128)} %multiply_reduce_fusion.4), channel_id=1, replica_groups=mesh['grid'=2,'rank'=4,'term'=4] {'grid','rank'}, use_global_device_ids=true, to_apply=%region_11.12 | all-reduce | flops 1 | bytes 8 | tf_op jit(solution)/shard_map/psum | solution.py:67
  174.8 0.6 multiply_reduce_fusion.3
  175.5 12.4 %psum.60 = f32[]{:T(128)} all-reduce(f32[]{:T(128)} %get-tuple-element.8), channel_id=1, replica_groups=mesh['grid'=2,'rank'=4,'term'=4] {'grid','rank'}, use_global_device_ids=true, to_apply=%region_13.14 | all-reduce | flops 1 | bytes 8 | tf_op jit(solution)/shard_map/psum | solution.py:50
  189.2 3.4 collective-permute-start.6
  192.6 1.3 collective-permute-start.7
  194.2 4.2 %collective-permute-done.7 = f32[32,1,256]{2,0,1:T(8,128)S(1)} collective-permute-done((f32[32,1,256]{2,0,1:T(8,128)S(1)}, f32[32,1,256]{2,0,1:T(8,128)S(1)}, u32[]{:S(2)}, u32[]{:S(2)}) %collective-permute-start.7) | collective-permute-done | bytes 32800 | tf_op jit(solution)/shard_map/ppermute | solution.py:17
  198.6 0.6 convolution_bitcast_fusion.1
  199.2 0.8 copy.77
  200.1 31.2 %all-reduce.19.cloned.1.call-done = f32[128,2,256]{2,1,0:T(2,128)} async-done(((f32[128,2,256]{2,1,0:T(2,128)}), f32[128,2,256]{2,1,0:T(2,128)}) %all-reduce.19.cloned.1.call-update) | async-done | bytes 262160
  231.3 0.8 constant_dynamic-slice_fusion.1
  232.2 13.9 %all-gather.2 = f32[128,2,256]{2,1,0:T(2,128)S(1)} all-gather(f32[32,2,256]{2,1,0:T(2,128)S(1)} %constant_dynamic-slice_fusion.1), channel_id=4, replica_groups=mesh['grid'=2,'rank'=4,'term'=4] {'term'}, dimensions={0}, use_global_device_ids=true | all-gather | bytes 327680 | tf_op jit(solution)/shard_map/all_gather | solution.py:65
  246.8 12.4 %psum.61 = f32[]{:T(128)} all-reduce(f32[]{:T(128)} %multiply_reduce_fusion.2), channel_id=1, replica_groups=mesh['grid'=2,'rank'=4,'term'=4] {'grid','rank'}, use_global_device_ids=true, to_apply=%region_17.18 | all-reduce | flops 1 | bytes 8 | tf_op jit(solution)/shard_map/psum | solution.py:67
  261.2 12.4 %psum.62 = f32[]{:T(128)} all-reduce(f32[]{:T(128)} %get-tuple-element.6), channel_id=1, replica_groups=mesh['grid'=2,'rank'=4,'term'=4] {'grid','rank'}, use_global_device_ids=true, to_apply=%region_19.20 | all-reduce | flops 1 | bytes 8 | tf_op jit(solution)/shard_map/psum | solution.py:50
  275.0 3.4 collective-permute-start.8
  278.4 1.3 collective-permute-start.9
  279.9 4.2 %collective-permute-done.9 = f32[32,1,256]{2,0,1:T(8,128)S(1)} collective-permute-done((f32[32,1,256]{2,0,1:T(8,128)S(1)}, f32[32,1,256]{2,0,1:T(8,128)S(1)}, u32[]{:S(2)}, u32[]{:S(2)}) %collective-permute-start.9) | collective-permute-done | bytes 32800 | tf_op jit(solution)/shard_map/ppermute | solution.py:17
  284.3 0.6 convolution_bitcast_fusion
  284.9 0.8 copy.79
  285.8 31.3 %all-reduce.21.cloned.1.call-done = f32[128,2,256]{2,1,0:T(2,128)} async-done(((f32[128,2,256]{2,1,0:T(2,128)}), f32[128,2,256]{2,1,0:T(2,128)}) %all-reduce.21.cloned.1.call-update) | async-done | bytes 262160
  317.1 0.8 constant_dynamic-slice_fusion
  317.9 13.9 %all-gather.3 = f32[128,2,256]{2,1,0:T(2,128)S(1)} all-gather(f32[32,2,256]{2,1,0:T(2,128)S(1)} %constant_dynamic-slice_fusion), channel_id=5, replica_groups=mesh['grid'=2,'rank'=4,'term'=4] {'term'}, dimensions={0}, use_global_device_ids=true | all-gather | bytes 327680 | tf_op jit(solution)/shard_map/all_gather | solution.py:65
  332.5 12.4 %psum.63 = f32[]{:T(128)} all-reduce(f32[]{:T(128)} %multiply_reduce_fusion), channel_id=1, replica_groups=mesh['grid'=2,'rank'=4,'term'=4] {'grid','rank'}, use_global_device_ids=true, to_apply=%region_23.24 | all-reduce | flops 1 | bytes 8 | tf_op jit(solution)/shard_map/psum | solution.py:67
  346.3 0.7 copy.82
  347.0 0.7 copy.81
  (63 shorter events, 6.9 us)
Async XLA Ops:
  7.2 18.8 %copy-start = (f32[3,32,128]{2,1,0:T(8,128)S(1)}, f32[3,32,128]{2,1,0:T(8,128)}, u32[]{:S(2)}) copy-start(f32[3,32,128]{2,1,0:T(8,128)} %param.5) | copy-start | bytes 147460
  7.2 52.7 %all-reduce.15.cloned.1.call-start = ((), (), s32[]{:S(2)}) async-start(), calls=%async_computation | async-start | bytes 524288
  8.0 13.0 %collective-permute-start.1 = (f32[3,1,256]{2,1,0:T(1,128)S(1)}, f32[3,1,256]{2,1,0:T(1,128)S(1)}, u32[]{:S(2)}, u32[]{:S(2)}) collective-permute-start(f32[3,1,256]{2,1,0:T(1,128)S(1)} %get-tuple-element.47), channel_id=1, source_target_pairs={{0,16},{1,17},{2,18},{3,19},{4,20},{5,21},{6,22},{7,23},{8,24},{9,... | collective-permute-start | bytes 9224 | tf_op jit(solution)/shard_map/ppermute | solution.py:14
  12.8 8.2 %collective-permute-start = (f32[3,1,256]{2,1,0:T(1,128)S(1)}, f32[3,1,256]{2,1,0:T(1,128)S(1)}, u32[]{:S(2)}, u32[]{:S(2)}) collective-permute-start(f32[3,1,256]{2,1,0:T(1,128)S(1)} %get-tuple-element.48), channel_id=1, source_target_pairs={{16,0},{17,1},{18,2},{19,3},{20,4},{21,5},{22,6},{23,7},{24,8},{25... | collective-permute-start | bytes 9224 | tf_op jit(solution)/shard_map/ppermute | solution.py:17
  14.1 6.9 %copy-start.2 = (f32[3,2,256]{2,1,0:T(2,128)S(1)}, f32[3,2,256]{2,1,0:T(2,128)}, u32[]{:S(2)}) copy-start(f32[3,2,256]{2,1,0:T(2,128)} %param.4) | copy-start | bytes 18436
  15.1 6.1 %collective-permute-start.2 = (f32[32,1,256]{2,1,0:T(1,128)S(1)}, f32[32,1,256]{2,1,0:T(1,128)S(1)}, u32[]{:S(2)}, u32[]{:S(2)}) collective-permute-start(f32[32,1,256]{2,1,0:T(1,128)S(1)} %get-tuple-element.45), channel_id=1, source_target_pairs={{0,16},{1,17},{2,18},{3,19},{4,20},{5,21},{6,22},{7,23},{8,24},{9,... | collective-permute-start | bytes 98312 | tf_op jit(solution)/shard_map/ppermute | solution.py:14
  19.7 5.8 %collective-permute-start.3 = (f32[32,1,256]{2,1,0:T(1,128)S(1)}, f32[32,1,256]{2,1,0:T(1,128)S(1)}, u32[]{:S(2)}, u32[]{:S(2)}) collective-permute-start(f32[32,1,256]{2,1,0:T(1,128)S(1)} %get-tuple-element.46), channel_id=1, source_target_pairs={{16,0},{17,1},{18,2},{19,3},{20,4},{21,5},{22,6},{23,7},{24,8},{25... | collective-permute-start | bytes 98312 | tf_op jit(solution)/shard_map/ppermute | solution.py:17
  21.1 4.4 %copy-start.1 = (f32[32,2,256]{2,1,0:T(2,128)S(1)}, f32[32,2,256]{2,1,0:T(2,128)}, u32[]{:S(2)}) copy-start(f32[32,2,256]{2,1,0:T(2,128)} %param.3) | copy-start | bytes 196612
  27.4 118.2 %all-reduce.17.cloned.1.call-start = ((), (), s32[]{:S(2)}) async-start(), calls=%async_computation.1 | async-start | bytes 524288
  27.5 0.7 copy-start.3
  103.5 5.0 %collective-permute-start.4 = (f32[32,1,256]{2,0,1:T(8,128)S(1)}, f32[32,1,256]{2,0,1:T(8,128)S(1)}, u32[]{:S(2)}, u32[]{:S(2)}) collective-permute-start(f32[32,1,256]{2,0,1:T(8,128)S(1)} %get-tuple-element.41), channel_id=1, source_target_pairs={{0,16},{1,17},{2,18},{3,19},{4,20},{5,21},{6,22},{7,23},{8,24},{9,... | collective-permute-start | bytes 98312 | tf_op jit(solution)/shard_map/ppermute | solution.py:14
  106.9 5.8 %collective-permute-start.5 = (f32[32,1,256]{2,0,1:T(8,128)S(1)}, f32[32,1,256]{2,0,1:T(8,128)S(1)}, u32[]{:S(2)}, u32[]{:S(2)}) collective-permute-start(f32[32,1,256]{2,0,1:T(8,128)S(1)} %get-tuple-element.42), channel_id=1, source_target_pairs={{16,0},{17,1},{18,2},{19,3},{20,4},{21,5},{22,6},{23,7},{24,8},{25... | collective-permute-start | bytes 98312 | tf_op jit(solution)/shard_map/ppermute | solution.py:17
  114.3 117.0 %all-reduce.19.cloned.1.call-start = ((), (), s32[]{:S(2)}) async-start(), calls=%async_computation.2 | async-start | bytes 524288
  189.2 5.0 %collective-permute-start.6 = (f32[32,1,256]{2,0,1:T(8,128)S(1)}, f32[32,1,256]{2,0,1:T(8,128)S(1)}, u32[]{:S(2)}, u32[]{:S(2)}) collective-permute-start(f32[32,1,256]{2,0,1:T(8,128)S(1)} %get-tuple-element.37), channel_id=1, source_target_pairs={{0,16},{1,17},{2,18},{3,19},{4,20},{5,21},{6,22},{7,23},{8,24},{9,... | collective-permute-start | bytes 98312 | tf_op jit(solution)/shard_map/ppermute | solution.py:14
  192.6 5.8 %collective-permute-start.7 = (f32[32,1,256]{2,0,1:T(8,128)S(1)}, f32[32,1,256]{2,0,1:T(8,128)S(1)}, u32[]{:S(2)}, u32[]{:S(2)}) collective-permute-start(f32[32,1,256]{2,0,1:T(8,128)S(1)} %get-tuple-element.38), channel_id=1, source_target_pairs={{16,0},{17,1},{18,2},{19,3},{20,4},{21,5},{22,6},{23,7},{24,8},{25... | collective-permute-start | bytes 98312 | tf_op jit(solution)/shard_map/ppermute | solution.py:17
  200.1 117.0 %all-reduce.21.cloned.1.call-start = ((), (), s32[]{:S(2)}) async-start(), calls=%async_computation.3 | async-start | bytes 524288
  275.0 5.0 %collective-permute-start.8 = (f32[32,1,256]{2,0,1:T(8,128)S(1)}, f32[32,1,256]{2,0,1:T(8,128)S(1)}, u32[]{:S(2)}, u32[]{:S(2)}) collective-permute-start(f32[32,1,256]{2,0,1:T(8,128)S(1)} %get-tuple-element.33), channel_id=1, source_target_pairs={{0,16},{1,17},{2,18},{3,19},{4,20},{5,21},{6,22},{7,23},{8,24},{9,... | collective-permute-start | bytes 98312 | tf_op jit(solution)/shard_map/ppermute | solution.py:14
  278.4 5.8 %collective-permute-start.9 = (f32[32,1,256]{2,0,1:T(8,128)S(1)}, f32[32,1,256]{2,0,1:T(8,128)S(1)}, u32[]{:S(2)}, u32[]{:S(2)}) collective-permute-start(f32[32,1,256]{2,0,1:T(8,128)S(1)} %get-tuple-element.34), channel_id=1, source_target_pairs={{16,0},{17,1},{18,2},{19,3},{20,4},{21,5},{22,6},{23,7},{24,8},{25... | collective-permute-start | bytes 98312 | tf_op jit(solution)/shard_map/ppermute | solution.py:17
Sparse Core Ops, SparseCore 0:
  27.6 32.2 all-reduce.14
  114.5 31.1 all-reduce.16
  200.2 31.0 all-reduce.18
  285.9 31.1 all-reduce.20
